TPU v7x, 512 devices: a whole 4x4x16 slice. The times are simulated.
512 devices in a mesh: dp: 32 (over x, z_lo), tile: 16 (over z_hi, y, core).
Axes of the slice: x: 4, y: 4, z: 16 (z_hi: 2, z_lo: 8; z = z_hi * 8 + z_lo), core: 2. Of those that a mesh axis runs over, the one named last changes fastest.
Arguments:
- tokens: bfloat16 [32, 16, 16, 16, 384], P('dp', 'tile'), may hold values from -1.5 to 1.5
- timesteps: int32 [32], P('dp'), may hold values from 0 to 999
- cond_weight: bfloat16 [256, 384], replicated, may hold values from -0.375 to 0.375
- qkv_weight: bfloat16 [384, 1152], replicated, may hold values from -0.3125 to 0.3125
- head_scale: float32 [6], replicated, may hold values from 4 to 20
- out_weight: bfloat16 [384, 384], replicated, may hold values from -0.875 to 0.875
- cotangent: bfloat16 [32, 16, 16, 16, 384], P('dp', 'tile'), may hold values from -0.015625 to 0.015625
Outputs:
- updated: bfloat16 [32, 16, 16, 16, 384], P('dp', 'tile')
- grad_out_weight: float32 [384, 384], replicated
All inputs are finite; a program needn't handle non-finite values.
Results may differ from a plain program's by a relative error of at most 0.015.
Values may be sent and summed in bfloat16 or wider, within the bound.
A program may use at most 64 MiB of HBM per device.

v0:
```python
import math

import jax
import jax.numpy as jnp
from jax import lax
from jax.sharding import PartitionSpec as P


def passed_along(x, axis, by):
    length = lax.axis_size(axis)
    pairs = [(i, i + by) for i in range(length) if 0 <= i + by < length]
    return lax.ppermute(x, axis, pairs)


def normalize(vectors):
    return vectors / jnp.sqrt(jnp.sum(vectors * vectors, axis=-1, keepdims=True) + 1e-06)


def extend_rims(block, grid_count, grid_col):
    tile_side = block.shape[0]
    west_rim = passed_along(block[:, tile_side - 3 :], "tile", 1)
    east_rim = passed_along(block[:, :3], "tile", -1)
    west_rim = jnp.where(grid_col > 0, west_rim, jnp.zeros_like(west_rim))
    east_rim = jnp.where(grid_col < grid_count - 1, east_rim, jnp.zeros_like(east_rim))
    widened = jnp.concatenate([west_rim, block, east_rim], axis=1)
    north_rim = passed_along(widened[tile_side - 3 :], "tile", grid_count)
    south_rim = passed_along(widened[:3], "tile", -grid_count)
    return jnp.concatenate([north_rim, widened, south_rim], axis=0)


def body(tokens, timesteps, cond_weight, qkv_weight, head_scale, out_weight, cotangent):
    tile_count = lax.axis_size("tile")
    grid_count = math.isqrt(tile_count)
    tile_place = lax.axis_index("tile")
    grid_row = tile_place // grid_count
    grid_col = tile_place % grid_count
    tile_side = tokens.shape[2]
    width = tokens.shape[4]
    head_count = head_scale.shape[0]
    head_dim = width // head_count
    padded_side = tile_side + 6
    image_side = grid_count * tile_side
    half_count = cond_weight.shape[0] // 2
    frequency = jnp.exp(-math.log(10000.0) * jnp.arange(half_count, dtype=jnp.float32) / half_count)
    angles = timesteps.astype(jnp.float32)[:, None] * frequency[None, :]
    features = jnp.concatenate([jnp.cos(angles), jnp.sin(angles)], axis=1)
    norm_gain = 1.0 + jnp.dot(
        features, cond_weight.astype(jnp.float32), precision=lax.Precision.HIGHEST
    )
    image_rows = tokens[0, 0].astype(jnp.float32)
    mean_square = jnp.mean(image_rows * image_rows, axis=-1, keepdims=True)
    normed = (image_rows * lax.rsqrt(mean_square + 1e-06) * norm_gain[0]).astype(jnp.bfloat16)
    flat_normed = normed.reshape(-1, width)
    projected = jnp.dot(flat_normed, qkv_weight, preferred_element_type=jnp.float32)
    queries = projected[:, :width]
    key_local = (
        normalize(projected[:, width : 2 * width].reshape(-1, head_count, head_dim))
        .astype(jnp.bfloat16)
        .reshape(tile_side, tile_side, width)
    )
    value_local = (
        projected[:, 2 * width :].astype(jnp.bfloat16).reshape(tile_side, tile_side, width)
    )
    padded = extend_rims(jnp.concatenate([key_local, value_local], axis=-1), grid_count, grid_col)
    key_rows = padded[:, :, :width].reshape(padded_side, padded_side, head_count, head_dim)
    value_rows = padded[:, :, width:].reshape(padded_side, padded_side, head_count, head_dim)
    query_unit = normalize(queries.reshape(tile_side, tile_side, head_count, head_dim)).astype(
        jnp.bfloat16
    )
    block_rows = 1
    for candidate in range(1, tile_side + 1):
        if tile_side % candidate == 0 and candidate <= max(1, 512 // tile_side):
            block_rows = candidate
    query_block = query_unit.reshape(-1, head_count, head_dim)
    key_block = key_rows.reshape(-1, head_count, head_dim)
    value_block = value_rows.reshape(-1, head_count, head_dim)
    scores = (
        jnp.einsum("qhd,khd->hqk", query_block, key_block, preferred_element_type=jnp.float32)
        * head_scale[:, None, None]
    )
    query_index = jnp.arange(block_rows * tile_side, dtype=jnp.int32)
    key_index = jnp.arange((block_rows + 6) * padded_side, dtype=jnp.int32)
    query_y = grid_row * tile_side + 0 + query_index // tile_side
    query_x = grid_col * tile_side + query_index % tile_side
    key_y = grid_row * tile_side + 0 + key_index // padded_side - 3
    key_x = grid_col * tile_side + key_index % padded_side - 3
    key_inside = (key_y >= 0) & (key_y < image_side) & (key_x >= 0) & (key_x < image_side)
    allowed = (
        key_inside[None, :]
        & (jnp.abs(key_y[None, :] - query_y[:, None]) <= 3)
        & (jnp.abs(key_x[None, :] - query_x[:, None]) <= 3)
    )
    expscore = jnp.where(allowed[None], jnp.exp(scores), 0.0)
    weight = (expscore / jnp.sum(expscore, axis=-1, keepdims=True)).astype(jnp.bfloat16)
    result_block = jnp.einsum(
        "hqk,khd->qhd", weight, value_block, preferred_element_type=jnp.float32
    )
    pieces = result_block.reshape(-1, width)
    attended = pieces.astype(jnp.bfloat16)
    branch = jnp.dot(attended, out_weight, preferred_element_type=jnp.float32)
    updated = (image_rows.reshape(-1, width) + branch).astype(jnp.bfloat16).reshape(tokens.shape)
    cot_rows = cotangent[0, 0].reshape(-1, width)
    grad_local = jnp.einsum("nc,nd->cd", attended, cot_rows, preferred_element_type=jnp.float32)
    grad_out_weight = lax.psum(grad_local, ("dp", "tile"))
    return (updated, grad_out_weight)


def solution(mesh):
    return jax.shard_map(
        body,
        mesh=mesh,
        in_specs=(
            P("dp", "tile", None, None, None),
            P("dp"),
            P(),
            P(),
            P(),
            P(),
            P("dp", "tile", None, None, None),
        ),
        out_specs=(P("dp", "tile", None, None, None), P()),
        check_vma=False,
    )
```

profile of v0, /device:TPU:1, one launch (start us, length us, event | category | flops | bytes accessed | tf_op | source)
XLA Modules:
  0.0 538.2 jit_solution(14227927429614082633)
XLA Ops:
  7.2 0.0 copy-start
  7.2 0.0 all-reduce.2.cloned.1.call-start
  7.9 0.1 fusion.29
  8.0 1.1 convolution_reduce_fusion
  9.1 1.0 multiply_reduce_fusion
  10.2 0.1 rsqrt.12
  10.3 1.0 fusion.10
  11.3 0.0 copy-done
  11.3 0.5 fusion.34
  11.8 0.1 slice_multiply_fusion
  12.0 0.2 copy.16
  12.2 0.1 copy.17
  12.3 0.3 div.73
  12.7 1.0 div.74
  13.7 1.1 divide_convert_fusion.5
  14.7 0.1 pad_maximum_fusion.6
  14.8 4.6 collective-permute-start
  19.4 5.5 %collective-permute-start.1 = (bf16[16,3,768]{2,1,0:T(4,128)(2,1)S(1)}, bf16[16,3,768]{2,1,0:T(4,128)(2,1)S(1)}, u32[]{:S(2)}, u32[]{:S(2)}) collective-permute-start(bf16[16,3,768]{2,1,0:T(4,128)(2,1)S(1)} %get-tuple-element.11), channel_id=1, source_target_pairs={{1,0},{2,1},{3,2},{4,3},{5,4},{6,5},{7,6},{8,7},{9,8},{10,9},{11,1... | collective-permute-start | bytes 221192 | tf_op jit(solution)/shard_map/ppermute | solution.py:12
  25.0 0.2 mul.89
  25.2 0.3 reduce_sum.38
  25.6 0.0 collective-permute-done
  25.7 0.2 collective-permute-done.1
  25.9 0.1 pad_maximum_fusion.4
  26.0 4.0 collective-permute-start.2
  30.1 1.3 collective-permute-start.3
  31.4 1.0 fusion.8
  32.3 0.1 copy.19
  32.4 0.9 copy.18
  33.3 0.0 copy-start.4
  33.3 0.0 copy-start.6
  33.3 0.0 collective-permute-done.2
  33.3 14.3 %collective-permute-done.3 = bf16[3,22,768]{2,1,0:T(8,128)(2,1)S(1)} collective-permute-done((bf16[3,22,768]{2,1,0:T(8,128)(2,1)S(1)}, bf16[3,22,768]{2,1,0:T(8,128)(2,1)S(1)}, u32[]{:S(2)}, u32[]{:S(2)}) %collective-permute-start.3) | collective-permute-done | bytes 101408 | tf_op jit(solution)/shard_map/ppermute | solution.py:12
  47.7 0.3 pad_maximum_fusion
  48.0 0.1 fusion.33
  48.1 0.6 reshape_reshape.7
  48.6 0.6 reshape_reshape.6
  49.2 0.0 copy-start.5
  49.2 0.0 copy-done.4
  49.2 0.0 copy-done.6
  49.2 1.8 fusion
  51.1 0.0 copy-done.5
  51.1 0.0 copy-start.3
  51.1 0.0 copy-start.1
  51.1 0.0 copy-start.2
  51.1 0.9 fusion.2
  52.1 0.0 copy-done.3
  52.1 1.1 fusion.35
  53.1 0.0 all-reduce.2.cloned.1.call-update
  53.2 0.0 copy-done.1
  53.2 0.0 copy-done.2
  53.2 1.0 fusion.3
  54.2 475.2 %all-reduce.2.cloned.1.call-done = f32[384,384]{1,0:T(8,128)} async-done(((f32[384,384]{1,0:T(8,128)}), f32[384,384]{1,0:T(8,128)}) %all-reduce.2.cloned.1.call-update) | async-done | bytes 589840 | tf_op jit(solution)/shard_map/psum | solution.py:104
  529.4 1.9 copy.30
  (11 shorter events, 0.2 us)
Async XLA Ops:
  7.2 4.2 copy-start
  7.2 522.2 %all-reduce.2.cloned.1.call-start = ((), (), s32[]{:S(2)}) async-start(), calls=%async_computation | async-start | bytes 1179648 | tf_op jit(solution)/shard_map/psum | solution.py:104
  14.8 10.8 %collective-permute-start = (bf16[16,3,768]{2,1,0:T(4,128)(2,1)S(1)}, bf16[16,3,768]{2,1,0:T(4,128)(2,1)S(1)}, u32[]{:S(2)}, u32[]{:S(2)}) collective-permute-start(bf16[16,3,768]{2,1,0:T(4,128)(2,1)S(1)} %get-tuple-element.10), channel_id=1, source_target_pairs={{0,1},{1,2},{2,3},{3,4},{4,5},{5,6},{6,7},{7,8},{8,9},{9,10},{10,1... | collective-permute-start | bytes 221192 | tf_op jit(solution)/shard_map/ppermute | solution.py:12
  19.4 6.4 %collective-permute-start.1 = (bf16[16,3,768]{2,1,0:T(4,128)(2,1)S(1)}, bf16[16,3,768]{2,1,0:T(4,128)(2,1)S(1)}, u32[]{:S(2)}, u32[]{:S(2)}) collective-permute-start(bf16[16,3,768]{2,1,0:T(4,128)(2,1)S(1)} %get-tuple-element.11), channel_id=1, source_target_pairs={{1,0},{2,1},{3,2},{4,3},{5,4},{6,5},{7,6},{8,7},{9,8},{10,9},{11,1... | collective-permute-start | bytes 221192 | tf_op jit(solution)/shard_map/ppermute | solution.py:12
  26.0 7.3 %collective-permute-start.2 = (bf16[3,22,768]{2,1,0:T(8,128)(2,1)S(1)}, bf16[3,22,768]{2,1,0:T(8,128)(2,1)S(1)}, u32[]{:S(2)}, u32[]{:S(2)}) collective-permute-start(bf16[3,22,768]{2,1,0:T(8,128)(2,1)S(1)} %get-tuple-element.8), channel_id=1, source_target_pairs={{0,4},{1,5},{2,6},{3,7},{4,8},{5,9},{6,10},{7,11},{8,12},{9,13},{1... | collective-permute-start | bytes 304136 | tf_op jit(solution)/shard_map/ppermute | solution.py:12
  30.1 17.6 %collective-permute-start.3 = (bf16[3,22,768]{2,1,0:T(8,128)(2,1)S(1)}, bf16[3,22,768]{2,1,0:T(8,128)(2,1)S(1)}, u32[]{:S(2)}, u32[]{:S(2)}) collective-permute-start(bf16[3,22,768]{2,1,0:T(8,128)(2,1)S(1)} %get-tuple-element.9), channel_id=1, source_target_pairs={{4,0},{5,1},{6,2},{7,3},{8,4},{9,5},{10,6},{11,7},{12,8},{13,9},{1... | collective-permute-start | bytes 304136 | tf_op jit(solution)/shard_map/ppermute | solution.py:12
  33.3 15.9 %copy-start.4 = (pred[256,484]{0,1:T(8,128)(4,1)S(1)}, pred[256,484]{0,1:T(8,128)(4,1)}, u32[]{:S(2)}) copy-start(pred[256,484]{0,1:T(8,128)(4,1)} %fusion.8) | copy-start | bytes 371716
  33.3 15.9 %copy-start.6 = (f32[6]{0:T(128)S(1)}, f32[6]{0:T(128)}, u32[]{:S(2)}) copy-start(f32[6]{0:T(128)} %param.11) | copy-start | bytes 76
  49.2 1.9 copy-start.5
  51.1 1.0 copy-start.3
  51.1 2.1 copy-start.1
  51.1 2.1 copy-start.2
Sparse Core Ops, SparseCore 0:
  53.3 476.0 all-reduce.1
where the time goes:
time: 539 us; the launch traced here: 538 us
  waiting for transfers between devices  490 us (91%)
  starting transfers between devices  15.5 us (3%)
  between operations  15.1 us (3%)
  matrix products  6.46 us (1%)
  local copies, waits for them, and re-layouts  6.12 us (1%)
    psum x1, waiting for transfers between devices, body(): grad_out_weight = lax.psum(grad_local, ('dp', 'tile'))  475 us
    ppermute x4, starting transfers between devices, passed_along(): return lax.ppermute(x, axis, pairs)  15.4 us
    ppermute x4, waiting for transfers between devices, passed_along(): return lax.ppermute(x, axis, pairs)  14.5 us
  transfers between devices with their start and end apart: 5, of which 3 were waited for; matrix products, arithmetic and copies ran while one was open for 1% of the time, Pallas kernels for 0%

commit v1 on v0

v1 whole, which is shorter than its diff:
```python
import math

import jax
import jax.numpy as jnp
from jax import lax
from jax.experimental import pallas as pl
from jax.experimental.pallas import tpu as pltpu
from jax.sharding import PartitionSpec as P

MESH = pl.DeviceIdType.MESH
F32, BF16 = jnp.float32, jnp.bfloat16
TOKENS = 256
CH = 384
HALO = 256
ROWS = 16
OWNERS = 12
HALF = OWNERS * ROWS
FAR = -16384.0
SENDS = (
    (1, 0, 208, 48, 0),
    (-1, 0, 0, 48, 48),
    (0, 1, 0, 48, 96),
    (0, -1, 48, 48, 144),
    (1, 1, 96, 16, 192),
    (1, -1, 112, 16, 208),
    (-1, 1, 128, 16, 224),
    (-1, -1, 144, 16, 240),
)


def mm(a, b):
    return jnp.dot(a, b, preferred_element_type=F32)


def iota(shape, axis):
    return lax.broadcasted_iota(jnp.int32, shape, axis)


def thirds(m):
    return (m >= 3).astype(jnp.int32) + (m >= 6).astype(jnp.int32) + (m >= 9).astype(jnp.int32)


def pick_matrix():
    r = iota((160, TOKENS), 0)
    m48 = jnp.where(r >= 48, r - 48, r)
    side = (m48 % 16) * 16 + m48 // 16 + jnp.where(r < 48, 13, 0)
    m = r % 16
    third = thirds(m)
    corner = third * 16 + m - 3 * third + jnp.where(r < 128, 13 * 16, 0)
    corner = corner + jnp.where((r < 112) | ((r >= 128) & (r < 144)), 13, 0)
    corner = jnp.where(m < 9, corner, -1)
    wanted = jnp.where(r < 96, side, corner)
    return jnp.where(iota((160, TOKENS), 1) == wanted, 1.0, 0.0).astype(BF16)


def key_marks(kr, kc, known, base):
    f = iota(kr.shape, 1) - base
    apart = jnp.where(f < 16, jnp.abs(kr - f), jnp.abs(kc - (f - 16)))
    bad = (apart > 3) | jnp.logical_not(known)
    return jnp.where(bad & (f >= 0) & (f < 32), FAR, 0.0)


def own_places(shape):
    i = iota(shape, 0)
    return i // 16, i % 16


def halo_places(shape, grid_row, grid_col):
    j = iota(shape, 0)
    m = jnp.where(j >= 144, j - 144, jnp.where(j >= 96, j - 96, jnp.where(j >= 48, j - 48, j)))
    first, second = m // 16, m % 16
    c = j % 16
    third = thirds(c)
    rest = c - 3 * third
    kr = jnp.where(j < 48, first - 3, jnp.where(j < 96, first + 16, second))
    kc = jnp.where(j < 96, second, jnp.where(j < 144, first - 3, first + 16))
    corner = j >= 192
    kr = jnp.where(corner, third + jnp.where(j < 224, -3, 16), kr)
    west = (j < 208) | ((j >= 224) & (j < 240))
    kc = jnp.where(corner, rest + jnp.where(west, -3, 16), kc)
    known = jnp.logical_not(corner & (c >= 9))
    known = known & ((kr >= 0) | (grid_row > 0)) & ((kr < 16) | (grid_row < 3))
    known = known & ((kc >= 0) | (grid_col > 0)) & ((kc < 16) | (grid_col < 3))
    return kr, kc, known


def device(x, y, core, z):
    return (x * 8 + lax.rem(z, 8), (z // 8) * 8 + y * 2 + core)


def owner_of(k, core):
    x, rest = k // 3, lax.rem(k, 3)
    y = rest + jnp.where(rest >= x, 1, 0)
    return x, jnp.where(core == 0, y, 3 - y)


def owned_by(x, y, core):
    y = jnp.where(core == 0, y, 3 - y)
    return jnp.where(x == y, OWNERS, x * 3 + y - jnp.where(y > x, 1, 0))


def kernel(
    tok_hbm, cot_hbm, qkv_hbm, out_w_hbm, cond_hbm, scale_hbm, step_ref,
    upd_ref, grad_ref,
    tok, cot, qkv, out_w, cond, scale_ref, packed, halo, q_s, k_s, v_s, acc, att,
    own, cross, sent, part, z1, z2, gath,
    in_sem, halo_s, halo_r, cross_s, cross_r, s1, r1, sz1, rz1, sz2, rz2, s3, r3, s4, r4,
):
    dp, tile = lax.axis_index("dp"), lax.axis_index("tile")
    grid_row, grid_col = tile // 4, lax.rem(tile, 4)
    x, z = dp // 8, (tile // 8) * 8 + lax.rem(dp, 8)
    y, core = lax.rem(tile, 8) // 2, lax.rem(tile, 2)
    a, b = z // 4, lax.rem(z, 4)
    chip = x * 4 + y
    mine = owned_by(x, y, core)
    owns = mine < OWNERS
    partner = (dp, tile + 1 - 2 * core)

    loads = [
        pltpu.make_async_copy(src, dst, in_sem.at[i])
        for i, (src, dst) in enumerate(((tok_hbm, tok), (cond_hbm, cond), (qkv_hbm, qkv), (cot_hbm, cot), (out_w_hbm, out_w), (scale_hbm, scale_ref)))
    ]
    for load in loads:
        load.start()

    halo[...] = jnp.zeros_like(halo)
    barrier = pltpu.get_barrier_semaphore()

    def there(dr, dc):
        ok = True
        if dr:
            ok = (grid_row < 3) if dr > 0 else (grid_row > 0)
        if dc:
            right = (grid_col < 3) if dc > 0 else (grid_col > 0)
            ok = (ok & right) if dr else right
        return ok

    near = 0
    for dr, dc, _, _, _ in SENDS:
        ok = there(dr, dc)
        near = near + jnp.where(ok, 1, 0)

        @pl.when(ok)
        def _():
            pl.semaphore_signal(barrier, inc=1, device_id=(dp, tile + 4 * dr + dc), device_id_type=MESH)

    pl.semaphore_signal(barrier, inc=1, device_id=partner, device_id_type=MESH)
    for i in range(1, 4):
        pl.semaphore_signal(barrier, inc=1, device_id=device(x, y, core, a * 4 + lax.rem(b + i, 4)), device_id_type=MESH)
        pl.semaphore_signal(barrier, inc=1, device_id=device(x, y, core, lax.rem(a + i, 4) * 4 + b), device_id_type=MESH)

    def greet(i, _):
        c = lax.rem(chip + i, 16)
        pl.semaphore_signal(barrier, inc=1, device_id=device(c // 4, lax.rem(c, 4), core, z), device_id_type=MESH)
        return 0

    lax.fori_loop(1, 16, greet, 0)

    loads[0].wait()
    packed[...] = mm(pick_matrix(), tok[...]).astype(BF16)

    pl.semaphore_wait(barrier, 22 + near)

    def halo_copy(i):
        dr, dc, place, count, into = SENDS[i]
        source = tok if dc == 0 else packed
        return pltpu.make_async_remote_copy(
            src_ref=source.at[pl.ds(place, count)], dst_ref=halo.at[pl.ds(into, count)],
            send_sem=halo_s, recv_sem=halo_r.at[i], device_id=(dp, tile + 4 * dr + dc), device_id_type=MESH,
        )

    for i, (dr, dc, _, _, _) in enumerate(SENDS):
        @pl.when(there(dr, dc))
        def _():
            halo_copy(i).start()

    loads[1].wait()
    loads[5].wait()
    frequency = jnp.exp((-math.log(10000.0) / 128) * iota((8, 128), 1).astype(F32))
    angles = step_ref[0].astype(F32) * frequency
    features = jnp.concatenate([jnp.cos(angles), jnp.sin(angles)], axis=1)
    high = features.astype(BF16)
    rest = features - high.astype(F32)
    middle = rest.astype(BF16)
    low = (rest - middle.astype(F32)).astype(BF16)
    gain = 1.0 + mm(high, cond[...]) + mm(middle, cond[...]) + mm(low, cond[...])
    gain = gain[0:1]

    same_head = jnp.where((iota((128, 128), 0) < 64) == (iota((128, 128), 1) < 64), 1.0, 0.0).astype(BF16)
    same_head = jnp.concatenate([same_head, same_head], axis=0)

    def normed(rows):
        wide = rows.astype(F32)
        mean_square = jnp.mean(wide * wide, axis=-1, keepdims=True)
        return (wide * lax.rsqrt(mean_square + 1e-06) * gain).astype(BF16)

    def unit(vectors):
        square = vectors * vectors
        high = square.astype(BF16)
        low = (square - high.astype(F32)).astype(BF16)
        total = mm(jnp.concatenate([high, low], axis=1), same_head)
        return vectors * lax.rsqrt(total + 1e-06)

    left = iota((TOKENS, 128), 1) < 64

    def put_keys(rows, where, kr, kc, known):
        even, odd = key_marks(kr, kc, known, 64), key_marks(kr, kc, known, 0)
        for p in range(3):
            key = unit(mm(rows, qkv[:, CH + 128 * p:CH + 128 * (p + 1)]))
            k_s[p, 0, where] = jnp.where(left, key, even).astype(BF16)
            k_s[p, 1, where] = jnp.where(left, odd, key).astype(BF16)
            value = mm(rows, qkv[:, 2 * CH + 128 * p:2 * CH + 128 * (p + 1)])
            v_s[p, where, 0:128] = value.astype(BF16)
            v_s[p, where, 128:256] = jnp.ones((TOKENS, 128), BF16)

    def attend(p, e, where):
        score = lax.dot_general(q_s[p, e], k_s[p, e, where], (((1,), (1,)), ((), ())), preferred_element_type=F32)
        return mm(jnp.exp2(score).astype(BF16), v_s[p, where])

    loads[2].wait()
    mine_rows, halo_rows = slice(0, TOKENS), slice(TOKENS, TOKENS + HALO)
    rows = normed(tok[...])
    kr, kc = own_places((TOKENS, 128))
    f = iota((TOKENS, 128), 1)

    def query_marks(base):
        g = f - base
        hit = ((g >= 0) & (g < 16) & (g == kr)) | ((g >= 16) & (g < 32) & (g - 16 == kc))
        return jnp.where(hit, 1.0, 0.0)

    even, odd = query_marks(64), query_marks(0)
    for p in range(3):
        scales = jnp.where(left, scale_ref[2 * p], scale_ref[2 * p + 1]) * math.log2(math.e)
        query = unit(mm(rows, qkv[:, 128 * p:128 * (p + 1)])) * scales
        q_s[p, 0] = jnp.where(left, query, even).astype(BF16)
        q_s[p, 1] = jnp.where(left, odd, query).astype(BF16)
    put_keys(rows, mine_rows, kr, kc, kr >= 0)
    for p in range(3):
        for e in range(2):
            acc[p, e] = attend(p, e, mine_rows)

    for i, (dr, dc, _, _, _) in enumerate(SENDS):
        @pl.when(there(-dr, -dc))
        def _():
            halo_copy(i).wait_recv()

    put_keys(normed(halo[...]), halo_rows, *halo_places((HALO, 128), grid_row, grid_col))

    loads[3].wait()
    for i in range(3):
        p = jnp.where(core == 0, 2 - i, i)
        r0 = acc[p, 0] + attend(p, 0, halo_rows)
        r1_ = acc[p, 1] + attend(p, 1, halo_rows)
        pair = jnp.where(left, r0[:, :128] / r0[:, 128:], r1_[:, :128] / r1_[:, 128:]).astype(BF16)
        att[p] = pair
        grad = lax.dot_general(pair, cot[...], (((0,), (0,)), ((), ())), preferred_element_type=F32)
        if i == 0:
            into = pl.multiple_of(jnp.where(core == 0, 64, 0), 64)
            sent[0:128] = grad.astype(BF16)
            pltpu.make_async_remote_copy(
                src_ref=sent.at[pl.ds(0, 128)], dst_ref=cross.at[pl.ds(into, 128)],
                send_sem=cross_s, recv_sem=cross_r, device_id=partner, device_id_type=MESH,
            ).start()
        elif i == 1:
            upper, lower = grad[0:64], grad[64:128]
            sent[128:192] = jnp.where(core == 0, lower, upper).astype(BF16)
            into = pl.multiple_of(jnp.where(core == 0, 0, 128), 64)
            pltpu.make_async_remote_copy(
                src_ref=sent.at[pl.ds(128, 64)], dst_ref=cross.at[pl.ds(into, 64)],
                send_sem=cross_s, recv_sem=cross_r, device_id=partner, device_id_type=MESH,
            ).start()
            keep = pl.multiple_of(jnp.where(core == 0, 128, 0), 64)
            own[pl.ds(keep, 64)] = jnp.where(core == 0, upper, lower)
        else:
            keep = pl.multiple_of(jnp.where(core == 0, 0, 64), 64)
            own[pl.ds(keep, 128)] = grad
    pltpu.make_async_copy(cross, cross, cross_r).wait()
    pltpu.make_async_copy(cross, cross, cross_s).wait()
    sent[...] = (own[...] + cross[...].astype(F32)).astype(BF16)

    def to_owner(i, _):
        k = lax.rem(mine + i, OWNERS)
        ox, oy = owner_of(k, core)

        @pl.when(k != mine)
        def _():
            pltpu.make_async_remote_copy(
                src_ref=sent.at[pl.ds(pl.multiple_of(k * ROWS, ROWS), ROWS)], dst_ref=part.at[chip],
                send_sem=s1, recv_sem=r1, device_id=device(ox, oy, core, z), device_id_type=MESH,
            ).start()
        return 0

    lax.fori_loop(0, OWNERS, to_owner, 0)

    loads[4].wait()
    branch = mm(att[0], out_w[0:128]) + mm(att[1], out_w[128:256]) + mm(att[2], out_w[256:384])
    upd_ref[...] = (tok[...].astype(F32) + branch).astype(BF16)

    def total_of(ref, count):
        total = ref[0].astype(F32)
        for i in range(1, count):
            total = total + ref[i].astype(F32)
        return total.astype(BF16)

    @pl.when(owns)
    def _():
        part[chip] = sent[pl.ds(pl.multiple_of(mine * ROWS, ROWS), ROWS)]
        pltpu.make_async_copy(part.at[pl.ds(0, 15)], part.at[pl.ds(0, 15)], r1).wait()
        z1[b] = total_of(part, 16)
        for i in range(1, 4):
            pltpu.make_async_remote_copy(
                src_ref=z1.at[b], dst_ref=z1.at[b], send_sem=sz1, recv_sem=rz1,
                device_id=device(x, y, core, a * 4 + lax.rem(b + i, 4)), device_id_type=MESH,
            ).start()
        pltpu.make_async_copy(z1.at[pl.ds(0, 3)], z1.at[pl.ds(0, 3)], rz1).wait()
        z2[a] = total_of(z1, 4)
        for i in range(1, 4):
            pltpu.make_async_remote_copy(
                src_ref=z2.at[a], dst_ref=z2.at[a], send_sem=sz2, recv_sem=rz2,
                device_id=device(x, y, core, lax.rem(a + i, 4) * 4 + b), device_id_type=MESH,
            ).start()
        pltpu.make_async_copy(z2.at[pl.ds(0, 3)], z2.at[pl.ds(0, 3)], rz2).wait()
        row = pl.multiple_of(core * HALF + mine * ROWS, ROWS)
        gath[pl.ds(row, ROWS)] = total_of(z2, 4)

        def spread(i, _):
            c = lax.rem(chip + i, 16)
            pltpu.make_async_remote_copy(
                src_ref=gath.at[pl.ds(row, ROWS)], dst_ref=gath.at[pl.ds(row, ROWS)],
                send_sem=s3, recv_sem=r3.at[mine], device_id=device(c // 4, lax.rem(c, 4), core, z), device_id_type=MESH,
            ).start()
            return 0

        lax.fori_loop(1, 16, spread, 0)

    def forward(i, _):
        k = lax.rem(mine + i, OWNERS)
        block = gath.at[pl.ds(pl.multiple_of(core * HALF + k * ROWS, ROWS), ROWS)]

        @pl.when(k != mine)
        def _():
            pltpu.make_async_copy(block, block, r3.at[k]).wait()

        pltpu.make_async_remote_copy(
            src_ref=block, dst_ref=block, send_sem=s4, recv_sem=r4, device_id=partner, device_id_type=MESH,
        ).start()
        return 0

    lax.fori_loop(0, OWNERS, forward, 0)
    half = gath.at[pl.ds(0, HALF)]
    pltpu.make_async_copy(half, half, r4).wait()
    grad_ref[...] = gath[...].astype(F32)

    pltpu.make_async_copy(half, half, s4).wait()
    for i, (dr, dc, _, _, _) in enumerate(SENDS):
        @pl.when(there(dr, dc))
        def _():
            halo_copy(i).wait_send()

    @pl.when(owns)
    def _():
        pltpu.make_async_copy(sent.at[pl.ds(0, HALF - ROWS)], sent.at[pl.ds(0, HALF - ROWS)], s1).wait()
        pltpu.make_async_copy(z1.at[pl.ds(0, 3)], z1.at[pl.ds(0, 3)], sz1).wait()
        pltpu.make_async_copy(z2.at[pl.ds(0, 3)], z2.at[pl.ds(0, 3)], sz2).wait()
        pltpu.make_async_copy(part.at[pl.ds(0, 15)], part.at[pl.ds(0, 15)], s3).wait()

    @pl.when(jnp.logical_not(owns))
    def _():
        pltpu.make_async_copy(sent, sent, s1).wait()


def body(tokens, timesteps, cond_weight, qkv_weight, head_scale, out_weight, cotangent):
    anywhere = pl.BlockSpec(memory_space=pltpu.HBM)
    whole = pl.BlockSpec(memory_space=pltpu.VMEM)
    dma = pltpu.SemaphoreType.DMA
    updated, grad = pl.pallas_call(
        kernel,
        out_shape=(pltpu.VMEM((TOKENS, CH), BF16), pltpu.VMEM((CH, CH), F32)),
        in_specs=[anywhere] * 6 + [pl.BlockSpec(memory_space=pltpu.SMEM)],
        out_specs=(whole, whole),
        scratch_shapes=[
            pltpu.VMEM((TOKENS, CH), BF16),
            pltpu.VMEM((TOKENS, CH), BF16),
            pltpu.VMEM((CH, 3 * CH), BF16),
            pltpu.VMEM((CH, CH), BF16),
            pltpu.VMEM((256, CH), BF16),
            pltpu.SMEM((6,), F32),
            pltpu.VMEM((160, CH), BF16),
            pltpu.VMEM((HALO, CH), BF16),
            pltpu.VMEM((3, 2, TOKENS, 128), BF16),
            pltpu.VMEM((3, 2, TOKENS + HALO, 128), BF16),
            pltpu.VMEM((3, TOKENS + HALO, 256), BF16),
            pltpu.VMEM((3, 2, TOKENS, 256), F32),
            pltpu.VMEM((3, TOKENS, 128), BF16),
            pltpu.VMEM((HALF, CH), F32),
            pltpu.VMEM((HALF, CH), BF16),
            pltpu.VMEM((HALF, CH), BF16),
            pltpu.VMEM((16, ROWS, CH), BF16),
            pltpu.VMEM((4, ROWS, CH), BF16),
            pltpu.VMEM((4, ROWS, CH), BF16),
            pltpu.VMEM((CH, CH), BF16),
            dma((6,)), dma(()), dma((8,)),
        ] + [dma(())] * 9 + [dma((OWNERS,)), dma(()), dma(())],
        compiler_params=pltpu.CompilerParams(collective_id=0, has_side_effects=True, vmem_limit_bytes=40 * 2**20),
    )(*(
        pltpu.with_memory_space_constraint(array, pltpu.HBM)
        for array in (
            tokens.reshape(TOKENS, CH), cotangent.reshape(TOKENS, CH),
            qkv_weight, out_weight, cond_weight, head_scale,
        )
    ), timesteps)
    return updated.reshape(tokens.shape), grad


def solution(mesh):
    return jax.shard_map(
        body,
        mesh=mesh,
        in_specs=(
            P("dp", "tile", None, None, None),
            P("dp"),
            P(),
            P(),
            P(),
            P(),
            P("dp", "tile", None, None, None),
        ),
        out_specs=(P("dp", "tile", None, None, None), P()),
        check_vma=False,
    )
```

time: 539 us -> 59 us (0.11)
  waiting for transfers between devices: 490 us -> 0 us
  Pallas kernels: 0 us -> 56.1 us
  starting transfers between devices: 15.5 us -> 0 us
  between operations: 15.1 us -> 1.29 us
  matrix products: 6.46 us -> 0 us
    psum x1 -> x0, waiting for transfers between devices: 475 us -> none  [body(): grad_out_weight = lax.psum(grad_local, ('dp', 'tile'))]
    pallas_call x0 -> x1, Pallas kernels: none -> 56.1 us  [body(): pl.pallas_call(kernel, out_shape=(pltpu.VMEM((TOKENS, CH), BF16), pltpu.V...]
    ppermute x4 -> x0, starting transfers between devices: 15.4 us -> none  [passed_along(): return lax.ppermute(x, axis, pairs)]
    ppermute x4 -> x0, waiting for transfers between devices: 14.5 us -> none  [passed_along(): return lax.ppermute(x, axis, pairs)]
    dot_general x6 -> x0, matrix products: 6.46 us -> none  [the longest x1 1.84 us: body(): jnp.einsum('qhd,khd->hqk', query_block, key_block, preferred_element_type...]
  transfers between devices with their start and end apart: 5 -> 0, of which waited for: 3 -> 0; matrix products, arithmetic and copies ran while one was open for 1% -> 0% of each run, Pallas kernels for 0% -> 0%
where the time goes in v1:
time: 59 us; the launch traced here: 58.9 us
  Pallas kernels  56.1 us (95%)
  local copies, waits for them, and re-layouts  1.49 us (3%)
  between operations  1.29 us (2%)
    pallas_call x1, Pallas kernels, body(): pl.pallas_call(kernel, out_shape=(pltpu.VMEM((TOKENS, CH), BF16), pltpu.V...  56.1 us
    unnamed x2, local copies, waits for them, and re-layouts  1.49 us

profile of v1, /device:TPU:1, one launch (start us, length us, event | category | flops | bytes accessed | tf_op | source)
XLA Modules:
  0.0 58.9 jit_solution(7843957871332346103)
XLA Ops:
  1.3 56.1 %shard_map.86 = (bf16[256,384]{1,0:T(8,128)(2,1)S(1)}, f32[384,384]{1,0:T(8,128)S(1)}) custom-call(bf16[256,384]{1,0:T(8,128)(2,1)} %bitcast.4, bf16[256,384]{1,0:T(8,128)(2,1)} %bitcast.5, bf16[384,1152]{1,0:T(8,128)(2,1)} %qkv_hbm.1, bf16[384,384]{1,0:T(8,128)(2,1)} %out_w_hbm.1, bf16[256,384]{1,0:T(8,128)(2,1)} %cond_hbm.1, f32[6]{0:T(128)} %scale_hbm.1, ...), custom_call_target="tpu_custom_call" | custom-call | tf_op jit(solution)/shard_map/pallas_call | solution.py:376
  57.4 0.7 %copy.11 = bf16[1,1,16,16,384]{4,3,2,1,0:T(8,128)(2,1)} copy(bf16[1,1,16,16,384]{4,3,2,1,0:T(8,128)(2,1)S(1)} %bitcast.3) | data formatting | bytes 393216
  58.1 0.8 %copy.12 = f32[384,384]{1,0:T(8,128)} copy(f32[384,384]{1,0:T(8,128)S(1)} %get-tuple-element.7) | data formatting | bytes 1179648

commit v2 on v1

--- a/solution.py
+++ b/solution.py
@@ -11,20 +11,26 @@
 F32, BF16 = jnp.float32, jnp.bfloat16
 TOKENS = 256
 CH = 384
-HALO = 256
+HALO = 384
+PART = 128
+STRIP = 48
 ROWS = 16
 OWNERS = 12
 HALF = OWNERS * ROWS
 FAR = -16384.0
 SENDS = (
     (1, 0, 208, 48, 0),
-    (-1, 0, 0, 48, 48),
-    (0, 1, 0, 48, 96),
-    (0, -1, 48, 48, 144),
-    (1, 1, 96, 16, 192),
-    (1, -1, 112, 16, 208),
-    (-1, 1, 128, 16, 224),
-    (-1, -1, 144, 16, 240),
+    (-1, 0, 0, 48, 128),
+    (1, 1, 96, 16, 48),
+    (1, -1, 112, 16, 64),
+    (-1, 1, 128, 16, 176),
+    (-1, -1, 144, 16, 192),
+    (0, 1, 0, 48, 256),
+    (0, -1, 48, 48, 304),
+)
+
+STEPS = sorted(
+    ((i, j) for i in range(4) for j in range(4) if i or j), key=lambda s: (-min(s[0], 4 - s[0]) - min(s[1], 4 - s[1]), s)
 )
 
 
@@ -65,33 +71,29 @@
     return i // 16, i % 16
 
 
-def halo_places(shape, grid_row, grid_col):
-    j = iota(shape, 0)
-    m = jnp.where(j >= 144, j - 144, jnp.where(j >= 96, j - 96, jnp.where(j >= 48, j - 48, j)))
-    first, second = m // 16, m % 16
+def side_places(grid_col):
+    j = iota((PART, 128), 0)
+    west = j < 48
+    m = jnp.where(west, j, j - 48)
+    known = (j < 96) & ((west & (grid_col > 0)) | (jnp.logical_not(west) & (grid_col < 3)))
+    return m % 16, m // 16 + jnp.where(west, -3, 16), known
+
+
+def strip_places(top, grid_row, grid_col):
+    j = iota((PART, 128), 0)
     c = j % 16
     third = thirds(c)
-    rest = c - 3 * third
-    kr = jnp.where(j < 48, first - 3, jnp.where(j < 96, first + 16, second))
-    kc = jnp.where(j < 96, second, jnp.where(j < 144, first - 3, first + 16))
-    corner = j >= 192
-    kr = jnp.where(corner, third + jnp.where(j < 224, -3, 16), kr)
-    west = (j < 208) | ((j >= 224) & (j < 240))
-    kc = jnp.where(corner, rest + jnp.where(west, -3, 16), kc)
-    known = jnp.logical_not(corner & (c >= 9))
-    known = known & ((kr >= 0) | (grid_row > 0)) & ((kr < 16) | (grid_row < 3))
-    known = known & ((kc >= 0) | (grid_col > 0)) & ((kc < 16) | (grid_col < 3))
-    return kr, kc, known
+    corner, west = j >= 48, j < 64
+    kr = jnp.where(corner, third, j // 16) + jnp.where(top, -3, 16)
+    kc = jnp.where(corner, c - 3 * third + jnp.where(west, -3, 16), c)
+    known = (west & (grid_col > 0)) | (jnp.logical_not(west) & (grid_col < 3))
+    known = jnp.logical_not(corner) | (known & (c < 9) & (j < 80))
+    beyond = jnp.where(top, grid_row > 0, grid_row < 3)
+    return kr, kc, known & beyond
 
 
 def device(x, y, core, z):
     return (x * 8 + lax.rem(z, 8), (z // 8) * 8 + y * 2 + core)
-
-
-def owner_of(k, core):
-    x, rest = k // 3, lax.rem(k, 3)
-    y = rest + jnp.where(rest >= x, 1, 0)
-    return x, jnp.where(core == 0, y, 3 - y)
 
 
 def owned_by(x, y, core):
@@ -102,7 +104,7 @@
 def kernel(
     tok_hbm, cot_hbm, qkv_hbm, out_w_hbm, cond_hbm, scale_hbm, step_ref,
     upd_ref, grad_ref,
-    tok, cot, qkv, out_w, cond, scale_ref, packed, halo, q_s, k_s, v_s, acc, att,
+    tok, cot, qkv, out_w, cond, scale_ref, packed, halo, q_s, k_s, v_s, acc, att, early,
     own, cross, sent, part, z1, z2, gath,
     in_sem, halo_s, halo_r, cross_s, cross_r, s1, r1, sz1, rz1, sz2, rz2, s3, r3, s4, r4,
 ):
@@ -120,9 +122,6 @@
         pltpu.make_async_copy(src, dst, in_sem.at[i])
         for i, (src, dst) in enumerate(((tok_hbm, tok), (cond_hbm, cond), (qkv_hbm, qkv), (cot_hbm, cot), (out_w_hbm, out_w), (scale_hbm, scale_ref)))
     ]
-    for load in loads:
-        load.start()
-
     halo[...] = jnp.zeros_like(halo)
     barrier = pltpu.get_barrier_semaphore()
 
@@ -144,17 +143,15 @@
         def _():
             pl.semaphore_signal(barrier, inc=1, device_id=(dp, tile + 4 * dr + dc), device_id_type=MESH)
 
+    for load in loads:
+        load.start()
     pl.semaphore_signal(barrier, inc=1, device_id=partner, device_id_type=MESH)
     for i in range(1, 4):
         pl.semaphore_signal(barrier, inc=1, device_id=device(x, y, core, a * 4 + lax.rem(b + i, 4)), device_id_type=MESH)
         pl.semaphore_signal(barrier, inc=1, device_id=device(x, y, core, lax.rem(a + i, 4) * 4 + b), device_id_type=MESH)
 
-    def greet(i, _):
-        c = lax.rem(chip + i, 16)
-        pl.semaphore_signal(barrier, inc=1, device_id=device(c // 4, lax.rem(c, 4), core, z), device_id_type=MESH)
-        return 0
-
-    lax.fori_loop(1, 16, greet, 0)
+    for i, j in STEPS:
+        pl.semaphore_signal(barrier, inc=1, device_id=device(lax.rem(x + i, 4), lax.rem(y + j, 4), core, z), device_id_type=MESH)
 
     loads[0].wait()
     packed[...] = mm(pick_matrix(), tok[...]).astype(BF16)
@@ -201,24 +198,43 @@
         total = mm(jnp.concatenate([high, low], axis=1), same_head)
         return vectors * lax.rsqrt(total + 1e-06)
 
-    left = iota((TOKENS, 128), 1) < 64
-
-    def put_keys(rows, where, kr, kc, known):
-        even, odd = key_marks(kr, kc, known, 64), key_marks(kr, kc, known, 0)
+    def left_of(count):
+        return iota((count, 128), 1) < 64
+
+    def put_keys(rows, begin, places):
+        count = rows.shape[0]
+        where, left = slice(begin, begin + count), left_of(count)
+        even, odd = key_marks(*places, 64), key_marks(*places, 0)
         for p in range(3):
             key = unit(mm(rows, qkv[:, CH + 128 * p:CH + 128 * (p + 1)]))
             k_s[p, 0, where] = jnp.where(left, key, even).astype(BF16)
             k_s[p, 1, where] = jnp.where(left, odd, key).astype(BF16)
             value = mm(rows, qkv[:, 2 * CH + 128 * p:2 * CH + 128 * (p + 1)])
             v_s[p, where, 0:128] = value.astype(BF16)
-            v_s[p, where, 128:256] = jnp.ones((TOKENS, 128), BF16)
-
-    def attend(p, e, where):
-        score = lax.dot_general(q_s[p, e], k_s[p, e, where], (((1,), (1,)), ((), ())), preferred_element_type=F32)
-        return mm(jnp.exp2(score).astype(BF16), v_s[p, where])
+            v_s[p, where, 128:256] = jnp.ones((count, 128), BF16)
+
+    def attend(p, e, queries, begin, count):
+        keys = slice(begin, begin + count)
+        score = lax.dot_general(q_s[p, e, queries], k_s[p, e, keys], (((1,), (1,)), ((), ())), preferred_element_type=F32)
+        return mm(jnp.exp2(score).astype(BF16), v_s[p, keys])
+
+    def shares(r0, r1):
+        left = left_of(r0.shape[0])
+        return jnp.where(left, r0[:, :128] / r0[:, 128:], r1[:, :128] / r1[:, 128:]).astype(BF16)
+
+    def outer(rows, cots):
+        return lax.dot_general(rows, cots, (((0,), (0,)), ((), ())), preferred_element_type=F32)
+
+    def await_halo(steps, wanted):
+        for i, (dr, dc, _, _, _) in enumerate(SENDS):
+            if dr not in steps:
+                continue
+
+            @pl.when(there(-dr, -dc) & wanted(dr))
+            def _():
+                halo_copy(i).wait_recv()
 
     loads[2].wait()
-    mine_rows, halo_rows = slice(0, TOKENS), slice(TOKENS, TOKENS + HALO)
     rows = normed(tok[...])
     kr, kc = own_places((TOKENS, 128))
     f = iota((TOKENS, 128), 1)
@@ -229,68 +245,73 @@
         return jnp.where(hit, 1.0, 0.0)
 
     even, odd = query_marks(64), query_marks(0)
+    left = left_of(TOKENS)
     for p in range(3):
         scales = jnp.where(left, scale_ref[2 * p], scale_ref[2 * p + 1]) * math.log2(math.e)
         query = unit(mm(rows, qkv[:, 128 * p:128 * (p + 1)])) * scales
         q_s[p, 0] = jnp.where(left, query, even).astype(BF16)
         q_s[p, 1] = jnp.where(left, odd, query).astype(BF16)
-    put_keys(rows, mine_rows, kr, kc, kr >= 0)
+    put_keys(rows, 0, (kr, kc, kr >= 0))
+    every = slice(0, TOKENS)
     for p in range(3):
         for e in range(2):
-            acc[p, e] = attend(p, e, mine_rows)
-
-    for i, (dr, dc, _, _, _) in enumerate(SENDS):
-        @pl.when(there(-dr, -dc))
-        def _():
-            halo_copy(i).wait_recv()
-
-    put_keys(normed(halo[...]), halo_rows, *halo_places((HALO, 128), grid_row, grid_col))
+            acc[p, e] = attend(p, e, every, 0, TOKENS)
+
+    await_halo((0,), lambda dr: True)
+    put_keys(normed(halo[2 * PART:3 * PART]), TOKENS, side_places(grid_col))
+    for p in range(3):
+        for e in range(2):
+            acc[p, e] += attend(p, e, every, TOKENS, PART)
+
+    top_last = lax.rem(grid_row, 2) == 0
+    await_halo((-1, 1), lambda dr: top_last if dr < 0 else jnp.logical_not(top_last))
+    near_rows = pl.multiple_of(jnp.where(top_last, PART, 0), PART)
+    put_keys(normed(halo[pl.ds(near_rows, PART)]), TOKENS + PART, strip_places(jnp.logical_not(top_last), grid_row, grid_col))
+    near_queries = pl.ds(pl.multiple_of(jnp.where(top_last, TOKENS - STRIP, 0), 16), STRIP)
+    for p in range(3):
+        for e in range(2):
+            acc[p, e, near_queries] += attend(p, e, near_queries, TOKENS + PART, PART)
 
     loads[3].wait()
-    for i in range(3):
-        p = jnp.where(core == 0, 2 - i, i)
-        r0 = acc[p, 0] + attend(p, 0, halo_rows)
-        r1_ = acc[p, 1] + attend(p, 1, halo_rows)
-        pair = jnp.where(left, r0[:, :128] / r0[:, 128:], r1_[:, :128] / r1_[:, 128:]).astype(BF16)
-        att[p] = pair
-        grad = lax.dot_general(pair, cot[...], (((0,), (0,)), ((), ())), preferred_element_type=F32)
-        if i == 0:
-            into = pl.multiple_of(jnp.where(core == 0, 64, 0), 64)
-            sent[0:128] = grad.astype(BF16)
-            pltpu.make_async_remote_copy(
-                src_ref=sent.at[pl.ds(0, 128)], dst_ref=cross.at[pl.ds(into, 128)],
-                send_sem=cross_s, recv_sem=cross_r, device_id=partner, device_id_type=MESH,
-            ).start()
-        elif i == 1:
-            upper, lower = grad[0:64], grad[64:128]
-            sent[128:192] = jnp.where(core == 0, lower, upper).astype(BF16)
-            into = pl.multiple_of(jnp.where(core == 0, 0, 128), 64)
-            pltpu.make_async_remote_copy(
-                src_ref=sent.at[pl.ds(128, 64)], dst_ref=cross.at[pl.ds(into, 64)],
-                send_sem=cross_s, recv_sem=cross_r, device_id=partner, device_id_type=MESH,
-            ).start()
-            keep = pl.multiple_of(jnp.where(core == 0, 128, 0), 64)
-            own[pl.ds(keep, 64)] = jnp.where(core == 0, upper, lower)
-        else:
-            keep = pl.multiple_of(jnp.where(core == 0, 0, 64), 64)
-            own[pl.ds(keep, 128)] = grad
-    pltpu.make_async_copy(cross, cross, cross_r).wait()
-    pltpu.make_async_copy(cross, cross, cross_s).wait()
+    done = pl.ds(pl.multiple_of(jnp.where(top_last, STRIP, 0), 16), TOKENS - STRIP)
+    for p in range(3):
+        att[p] = shares(acc[p, 0], acc[p, 1])
+        early[p] = outer(att[p, done], cot[done])
+
+    far_rows = pl.multiple_of(jnp.where(top_last, 0, PART), PART)
+    far_queries = pl.ds(pl.multiple_of(jnp.where(top_last, 0, TOKENS - STRIP), 16), STRIP)
+    places = strip_places(top_last, grid_row, grid_col)
+    await_halo((-1, 1), lambda dr: jnp.logical_not(top_last) if dr < 0 else top_last)
+    put_keys(normed(halo[pl.ds(far_rows, PART)]), TOKENS + 2 * PART, places)
+    late = [
+        [acc[p, e, far_queries] + attend(p, e, far_queries, TOKENS + 2 * PART, PART) for e in range(2)] for p in range(3)
+    ]
+    pairs = [shares(*r) for r in late]
+    far_cot = cot[far_queries]
+    grads = [early[p] + outer(pairs[p], far_cot) for p in range(3)]
+    first = jnp.concatenate([grads[0], grads[1][0:64]], axis=0)
+    second = jnp.concatenate([grads[1][64:128], grads[2]], axis=0)
+    sent[...] = jnp.where(core == 0, second, first).astype(BF16)
+    over = pltpu.make_async_remote_copy(
+        src_ref=sent, dst_ref=cross, send_sem=cross_s, recv_sem=cross_r, device_id=partner, device_id_type=MESH,
+    )
+    over.start()
+    own[...] = jnp.where(core == 0, first, second)
+    for p in range(3):
+        att[p, far_queries] = pairs[p]
+    over.wait()
     sent[...] = (own[...] + cross[...].astype(F32)).astype(BF16)
 
-    def to_owner(i, _):
-        k = lax.rem(mine + i, OWNERS)
-        ox, oy = owner_of(k, core)
-
-        @pl.when(k != mine)
+    for i, j in STEPS:
+        ox, oy = lax.rem(x + i, 4), lax.rem(y + j, 4)
+        k = owned_by(ox, oy, core)
+
+        @pl.when(k < OWNERS)
         def _():
             pltpu.make_async_remote_copy(
                 src_ref=sent.at[pl.ds(pl.multiple_of(k * ROWS, ROWS), ROWS)], dst_ref=part.at[chip],
                 send_sem=s1, recv_sem=r1, device_id=device(ox, oy, core, z), device_id_type=MESH,
             ).start()
-        return 0
-
-    lax.fori_loop(0, OWNERS, to_owner, 0)
 
     loads[4].wait()
     branch = mm(att[0], out_w[0:128]) + mm(att[1], out_w[128:256]) + mm(att[2], out_w[256:384])
@@ -323,30 +344,24 @@
         row = pl.multiple_of(core * HALF + mine * ROWS, ROWS)
         gath[pl.ds(row, ROWS)] = total_of(z2, 4)
 
-        def spread(i, _):
-            c = lax.rem(chip + i, 16)
+        for i, j in STEPS:
             pltpu.make_async_remote_copy(
-                src_ref=gath.at[pl.ds(row, ROWS)], dst_ref=gath.at[pl.ds(row, ROWS)],
-                send_sem=s3, recv_sem=r3.at[mine], device_id=device(c // 4, lax.rem(c, 4), core, z), device_id_type=MESH,
+                src_ref=gath.at[pl.ds(row, ROWS)], dst_ref=gath.at[pl.ds(row, ROWS)], send_sem=s3,
+                recv_sem=r3.at[mine], device_id=device(lax.rem(x + i, 4), lax.rem(y + j, 4), core, z), device_id_type=MESH,
             ).start()
-            return 0
-
-        lax.fori_loop(1, 16, spread, 0)
-
-    def forward(i, _):
-        k = lax.rem(mine + i, OWNERS)
-        block = gath.at[pl.ds(pl.multiple_of(core * HALF + k * ROWS, ROWS), ROWS)]
-
-        @pl.when(k != mine)
+
+    for i, j in ((0, 0),) + tuple(reversed(STEPS)):
+        k = owned_by(lax.rem(x + i, 4), lax.rem(y + j, 4), core)
+
+        @pl.when(k < OWNERS)
         def _():
-            pltpu.make_async_copy(block, block, r3.at[k]).wait()
-
-        pltpu.make_async_remote_copy(
-            src_ref=block, dst_ref=block, send_sem=s4, recv_sem=r4, device_id=partner, device_id_type=MESH,
-        ).start()
-        return 0
-
-    lax.fori_loop(0, OWNERS, forward, 0)
+            block = gath.at[pl.ds(pl.multiple_of(core * HALF + k * ROWS, ROWS), ROWS)]
+            if i or j:
+                pltpu.make_async_copy(block, block, r3.at[k]).wait()
+            pltpu.make_async_remote_copy(
+                src_ref=block, dst_ref=block, send_sem=s4, recv_sem=r4, device_id=partner, device_id_type=MESH,
+            ).start()
+
     half = gath.at[pl.ds(0, HALF)]
     pltpu.make_async_copy(half, half, r4).wait()
     grad_ref[...] = gath[...].astype(F32)
@@ -367,6 +382,17 @@
     @pl.when(jnp.logical_not(owns))
     def _():
         pltpu.make_async_copy(sent, sent, s1).wait()
+
+
+def hand_over(upd_ref, grad_ref, upd_hbm, grad_hbm, sems):
+    copies = [
+        pltpu.make_async_copy(grad_ref, grad_hbm, sems.at[0]),
+        pltpu.make_async_copy(upd_ref, upd_hbm, sems.at[1]),
+    ]
+    for copy in copies:
+        copy.start()
+    for copy in copies:
+        copy.wait()
 
 
 def body(tokens, timesteps, cond_weight, qkv_weight, head_scale, out_weight, cotangent):
@@ -392,6 +418,7 @@
             pltpu.VMEM((3, TOKENS + HALO, 256), BF16),
             pltpu.VMEM((3, 2, TOKENS, 256), F32),
             pltpu.VMEM((3, TOKENS, 128), BF16),
+            pltpu.VMEM((3, 128, CH), F32),
             pltpu.VMEM((HALF, CH), F32),
             pltpu.VMEM((HALF, CH), BF16),
             pltpu.VMEM((HALF, CH), BF16),
@@ -409,6 +436,13 @@
             qkv_weight, out_weight, cond_weight, head_scale,
         )
     ), timesteps)
+    updated, grad = pl.pallas_call(
+        hand_over,
+        out_shape=(pltpu.HBM((TOKENS, CH), BF16), pltpu.HBM((CH, CH), F32)),
+        in_specs=[pl.BlockSpec(memory_space=pl.ANY)] * 2,
+        out_specs=(pl.BlockSpec(memory_space=pl.ANY),) * 2,
+        scratch_shapes=[dma((2,))],
+    )(pltpu.with_memory_space_constraint(updated, pltpu.VMEM), pltpu.with_memory_space_constraint(grad, pltpu.VMEM))
     return updated.reshape(tokens.shape), grad
 
 

time: 59 us -> 56.9 us (0.964)
  local copies, waits for them, and re-layouts: 1.49 us -> 0 us
  Pallas kernels: 56.1 us -> 55.5 us
    pallas_call x1, Pallas kernels: 56.1 us -> 54.6 us  [body(): pl.pallas_call(kernel, out_shape=(pltpu.VMEM((TOKENS, CH), BF16), pltpu.V...]
    unnamed x2 -> x0, local copies, waits for them, and re-layouts: 1.49 us -> none
    pallas_call x0 -> x1, Pallas kernels: none -> 0.89 us  [body(): pl.pallas_call(hand_over, out_shape=(pltpu.HBM((TOKENS, CH), BF16), pltpu...]
where the time goes in v2:
time: 56.9 us; the launch traced here: 56.8 us
  Pallas kernels  55.5 us (98%)
  between operations  1.28 us (2%)
    pallas_call x1, Pallas kernels, body(): pl.pallas_call(kernel, out_shape=(pltpu.VMEM((TOKENS, CH), BF16), pltpu.V...  54.6 us

profile of v2, /device:TPU:1, one launch (start us, length us, event | category | flops | bytes accessed | tf_op | source)
XLA Modules:
  0.0 56.8 jit_solution(3597145301475784104)
XLA Ops:
  1.3 54.6 %shard_map.86 = (bf16[256,384]{1,0:T(8,128)(2,1)S(1)}, f32[384,384]{1,0:T(8,128)S(1)}) custom-call(bf16[256,384]{1,0:T(8,128)(2,1)} %bitcast.3, bf16[256,384]{1,0:T(8,128)(2,1)} %bitcast.4, bf16[384,1152]{1,0:T(8,128)(2,1)} %qkv_hbm.1, bf16[384,384]{1,0:T(8,128)(2,1)} %out_w_hbm.1, bf16[256,384]{1,0:T(8,128)(2,1)} %cond_hbm.1, f32[6]{0:T(128)} %scale_hbm.1, ...), custom_call_target="tpu_custom_call" | custom-call | tf_op jit(solution)/shard_map/pallas_call | solution.py:402
  55.9 0.9 %shard_map.87 = (bf16[256,384]{1,0:T(8,128)(2,1)}, f32[384,384]{1,0:T(8,128)}) custom-call(bf16[256,384]{1,0:T(8,128)(2,1)S(1)} %get-tuple-element.6.upd_ref, f32[384,384]{1,0:T(8,128)S(1)} %get-tuple-element.7.grad_ref), custom_call_target="tpu_custom_call" | custom-call | tf_op jit(solution)/shard_map/pallas_call | solution.py:439

commit v3 on v2

--- a/solution.py
+++ b/solution.py
@@ -33,6 +33,8 @@
     ((i, j) for i in range(4) for j in range(4) if i or j), key=lambda s: (-min(s[0], 4 - s[0]) - min(s[1], 4 - s[1]), s)
 )
 
+ALONG = sorted(range(1, 16), key=lambda i: -min(i, 16 - i))
+
 
 def mm(a, b):
     return jnp.dot(a, b, preferred_element_type=F32)
@@ -105,14 +107,13 @@
     tok_hbm, cot_hbm, qkv_hbm, out_w_hbm, cond_hbm, scale_hbm, step_ref,
     upd_ref, grad_ref,
     tok, cot, qkv, out_w, cond, scale_ref, packed, halo, q_s, k_s, v_s, acc, att, early,
-    own, cross, sent, part, z1, z2, gath,
-    in_sem, halo_s, halo_r, cross_s, cross_r, s1, r1, sz1, rz1, sz2, rz2, s3, r3, s4, r4,
+    own, cross, sent, part, z1, gath,
+    in_sem, halo_s, halo_r, cross_s, cross_r, s1, r1, sz1, rz1, s3, r3, s4, r4,
 ):
     dp, tile = lax.axis_index("dp"), lax.axis_index("tile")
     grid_row, grid_col = tile // 4, lax.rem(tile, 4)
     x, z = dp // 8, (tile // 8) * 8 + lax.rem(dp, 8)
     y, core = lax.rem(tile, 8) // 2, lax.rem(tile, 2)
-    a, b = z // 4, lax.rem(z, 4)
     chip = x * 4 + y
     mine = owned_by(x, y, core)
     owns = mine < OWNERS
@@ -146,17 +147,15 @@
     for load in loads:
         load.start()
     pl.semaphore_signal(barrier, inc=1, device_id=partner, device_id_type=MESH)
-    for i in range(1, 4):
-        pl.semaphore_signal(barrier, inc=1, device_id=device(x, y, core, a * 4 + lax.rem(b + i, 4)), device_id_type=MESH)
-        pl.semaphore_signal(barrier, inc=1, device_id=device(x, y, core, lax.rem(a + i, 4) * 4 + b), device_id_type=MESH)
-
+    for i in ALONG:
+        pl.semaphore_signal(barrier, inc=1, device_id=device(x, y, core, lax.rem(z + i, 16)), device_id_type=MESH)
     for i, j in STEPS:
         pl.semaphore_signal(barrier, inc=1, device_id=device(lax.rem(x + i, 4), lax.rem(y + j, 4), core, z), device_id_type=MESH)
 
     loads[0].wait()
     packed[...] = mm(pick_matrix(), tok[...]).astype(BF16)
 
-    pl.semaphore_wait(barrier, 22 + near)
+    pl.semaphore_wait(barrier, 31 + near)
 
     def halo_copy(i):
         dr, dc, place, count, into = SENDS[i]
@@ -327,22 +326,15 @@
     def _():
         part[chip] = sent[pl.ds(pl.multiple_of(mine * ROWS, ROWS), ROWS)]
         pltpu.make_async_copy(part.at[pl.ds(0, 15)], part.at[pl.ds(0, 15)], r1).wait()
-        z1[b] = total_of(part, 16)
-        for i in range(1, 4):
+        z1[z] = total_of(part, 16)
+        for i in ALONG:
             pltpu.make_async_remote_copy(
-                src_ref=z1.at[b], dst_ref=z1.at[b], send_sem=sz1, recv_sem=rz1,
-                device_id=device(x, y, core, a * 4 + lax.rem(b + i, 4)), device_id_type=MESH,
+                src_ref=z1.at[z], dst_ref=z1.at[z], send_sem=sz1, recv_sem=rz1,
+                device_id=device(x, y, core, lax.rem(z + i, 16)), device_id_type=MESH,
             ).start()
-        pltpu.make_async_copy(z1.at[pl.ds(0, 3)], z1.at[pl.ds(0, 3)], rz1).wait()
-        z2[a] = total_of(z1, 4)
-        for i in range(1, 4):
-            pltpu.make_async_remote_copy(
-                src_ref=z2.at[a], dst_ref=z2.at[a], send_sem=sz2, recv_sem=rz2,
-                device_id=device(x, y, core, lax.rem(a + i, 4) * 4 + b), device_id_type=MESH,
-            ).start()
-        pltpu.make_async_copy(z2.at[pl.ds(0, 3)], z2.at[pl.ds(0, 3)], rz2).wait()
+        pltpu.make_async_copy(z1.at[pl.ds(0, 15)], z1.at[pl.ds(0, 15)], rz1).wait()
         row = pl.multiple_of(core * HALF + mine * ROWS, ROWS)
-        gath[pl.ds(row, ROWS)] = total_of(z2, 4)
+        gath[pl.ds(row, ROWS)] = total_of(z1, 16)
 
         for i, j in STEPS:
             pltpu.make_async_remote_copy(
@@ -363,8 +355,11 @@
             ).start()
 
     half = gath.at[pl.ds(0, HALF)]
+    kept = pl.ds(pl.multiple_of(core * HALF, ROWS), HALF)
+    grad_ref[kept] = gath[kept].astype(F32)
     pltpu.make_async_copy(half, half, r4).wait()
-    grad_ref[...] = gath[...].astype(F32)
+    given = pl.ds(pl.multiple_of((1 - core) * HALF, ROWS), HALF)
+    grad_ref[given] = gath[given].astype(F32)
 
     pltpu.make_async_copy(half, half, s4).wait()
     for i, (dr, dc, _, _, _) in enumerate(SENDS):
@@ -375,8 +370,7 @@
     @pl.when(owns)
     def _():
         pltpu.make_async_copy(sent.at[pl.ds(0, HALF - ROWS)], sent.at[pl.ds(0, HALF - ROWS)], s1).wait()
-        pltpu.make_async_copy(z1.at[pl.ds(0, 3)], z1.at[pl.ds(0, 3)], sz1).wait()
-        pltpu.make_async_copy(z2.at[pl.ds(0, 3)], z2.at[pl.ds(0, 3)], sz2).wait()
+        pltpu.make_async_copy(z1.at[pl.ds(0, 15)], z1.at[pl.ds(0, 15)], sz1).wait()
         pltpu.make_async_copy(part.at[pl.ds(0, 15)], part.at[pl.ds(0, 15)], s3).wait()
 
     @pl.when(jnp.logical_not(owns))
@@ -423,11 +417,10 @@
             pltpu.VMEM((HALF, CH), BF16),
             pltpu.VMEM((HALF, CH), BF16),
             pltpu.VMEM((16, ROWS, CH), BF16),
-            pltpu.VMEM((4, ROWS, CH), BF16),
-            pltpu.VMEM((4, ROWS, CH), BF16),
+            pltpu.VMEM((16, ROWS, CH), BF16),
             pltpu.VMEM((CH, CH), BF16),
             dma((6,)), dma(()), dma((8,)),
-        ] + [dma(())] * 9 + [dma((OWNERS,)), dma(()), dma(())],
+        ] + [dma(())] * 7 + [dma((OWNERS,)), dma(()), dma(())],
         compiler_params=pltpu.CompilerParams(collective_id=0, has_side_effects=True, vmem_limit_bytes=40 * 2**20),
     )(*(
         pltpu.with_memory_space_constraint(array, pltpu.HBM)

time: 56.9 us -> 55.8 us (0.981)
  Pallas kernels: 55.5 us -> 54.3 us
    pallas_call x1, Pallas kernels: 54.6 us -> 53.5 us  [body(): pl.pallas_call(kernel, out_shape=(pltpu.VMEM((TOKENS, CH), BF16), pltpu.V...]
where the time goes in v3:
time: 55.8 us; the launch traced here: 55.6 us
  Pallas kernels  54.3 us (97%)
  between operations  1.28 us (2%)
    pallas_call x1, Pallas kernels, body(): pl.pallas_call(kernel, out_shape=(pltpu.VMEM((TOKENS, CH), BF16), pltpu.V...  53.5 us

profile of v3, /device:TPU:1, one launch (start us, length us, event | category | flops | bytes accessed | tf_op | source)
XLA Modules:
  0.0 55.6 jit_solution(15399392569481845385)
XLA Ops:
  1.3 53.5 %shard_map.86 = (bf16[256,384]{1,0:T(8,128)(2,1)S(1)}, f32[384,384]{1,0:T(8,128)S(1)}) custom-call(bf16[256,384]{1,0:T(8,128)(2,1)} %bitcast.3, bf16[256,384]{1,0:T(8,128)(2,1)} %bitcast.4, bf16[384,1152]{1,0:T(8,128)(2,1)} %qkv_hbm.1, bf16[384,384]{1,0:T(8,128)(2,1)} %out_w_hbm.1, bf16[256,384]{1,0:T(8,128)(2,1)} %cond_hbm.1, f32[6]{0:T(128)} %scale_hbm.1, ...), custom_call_target="tpu_custom_call" | custom-call | tf_op jit(solution)/shard_map/pallas_call | solution.py:396
  54.7 0.9 %shard_map.87 = (bf16[256,384]{1,0:T(8,128)(2,1)}, f32[384,384]{1,0:T(8,128)}) custom-call(bf16[256,384]{1,0:T(8,128)(2,1)S(1)} %get-tuple-element.6.upd_ref, f32[384,384]{1,0:T(8,128)S(1)} %get-tuple-element.7.grad_ref), custom_call_target="tpu_custom_call" | custom-call | tf_op jit(solution)/shard_map/pallas_call | solution.py:432

commit v4 on v3

--- a/solution.py
+++ b/solution.py
@@ -190,12 +190,15 @@
         mean_square = jnp.mean(wide * wide, axis=-1, keepdims=True)
         return (wide * lax.rsqrt(mean_square + 1e-06) * gain).astype(BF16)
 
-    def unit(vectors):
-        square = vectors * vectors
+    def units(wide):
+        count = wide.shape[0]
+        pairs = jnp.concatenate([wide[:, 128 * p:128 * (p + 1)] for p in range(3)], axis=0)
+        square = pairs * pairs
         high = square.astype(BF16)
         low = (square - high.astype(F32)).astype(BF16)
         total = mm(jnp.concatenate([high, low], axis=1), same_head)
-        return vectors * lax.rsqrt(total + 1e-06)
+        pairs = pairs * lax.rsqrt(total + 1e-06)
+        return [pairs[count * p:count * (p + 1)] for p in range(3)]
 
     def left_of(count):
         return iota((count, 128), 1) < 64
@@ -204,13 +207,12 @@
         count = rows.shape[0]
         where, left = slice(begin, begin + count), left_of(count)
         even, odd = key_marks(*places, 64), key_marks(*places, 0)
+        both = mm(rows, qkv[:, CH:3 * CH])
+        keys = units(both[:, :CH])
         for p in range(3):
-            key = unit(mm(rows, qkv[:, CH + 128 * p:CH + 128 * (p + 1)]))
-            k_s[p, 0, where] = jnp.where(left, key, even).astype(BF16)
-            k_s[p, 1, where] = jnp.where(left, odd, key).astype(BF16)
-            value = mm(rows, qkv[:, 2 * CH + 128 * p:2 * CH + 128 * (p + 1)])
-            v_s[p, where, 0:128] = value.astype(BF16)
-            v_s[p, where, 128:256] = jnp.ones((count, 128), BF16)
+            k_s[p, 0, where] = jnp.where(left, keys[p], even).astype(BF16)
+            k_s[p, 1, where] = jnp.where(left, odd, keys[p]).astype(BF16)
+            v_s[p, where, 0:128] = both[:, CH + 128 * p:CH + 128 * (p + 1)].astype(BF16)
 
     def attend(p, e, queries, begin, count):
         keys = slice(begin, begin + count)
@@ -245,9 +247,11 @@
 
     even, odd = query_marks(64), query_marks(0)
     left = left_of(TOKENS)
+    v_s[:, :, 128:256] = jnp.ones((3, TOKENS + HALO, 128), BF16)
+    queries = units(mm(rows, qkv[:, 0:CH]))
     for p in range(3):
         scales = jnp.where(left, scale_ref[2 * p], scale_ref[2 * p + 1]) * math.log2(math.e)
-        query = unit(mm(rows, qkv[:, 128 * p:128 * (p + 1)])) * scales
+        query = queries[p] * scales
         q_s[p, 0] = jnp.where(left, query, even).astype(BF16)
         q_s[p, 1] = jnp.where(left, odd, query).astype(BF16)
     put_keys(rows, 0, (kr, kc, kr >= 0))

time: 55.8 us -> 55.4 us (level)
  no operation moved by 1% of the time
where the time goes in v4:
time: 55.4 us; the launch traced here: 55.3 us
  Pallas kernels  54 us (97%)
  between operations  1.28 us (2%)
    pallas_call x1, Pallas kernels, body(): pl.pallas_call(kernel, out_shape=(pltpu.VMEM((TOKENS, CH), BF16), pltpu.V...  53.1 us

profile of v4, /device:TPU:1, one launch (start us, length us, event | category | flops | bytes accessed | tf_op | source)
XLA Modules:
  0.0 55.3 jit_solution(347824095457434513)
XLA Ops:
  1.3 53.1 %shard_map.86 = (bf16[256,384]{1,0:T(8,128)(2,1)S(1)}, f32[384,384]{1,0:T(8,128)S(1)}) custom-call(bf16[256,384]{1,0:T(8,128)(2,1)} %bitcast.3, bf16[256,384]{1,0:T(8,128)(2,1)} %bitcast.4, bf16[384,1152]{1,0:T(8,128)(2,1)} %qkv_hbm.1, bf16[384,384]{1,0:T(8,128)(2,1)} %out_w_hbm.1, bf16[256,384]{1,0:T(8,128)(2,1)} %cond_hbm.1, f32[6]{0:T(128)} %scale_hbm.1, ...), custom_call_target="tpu_custom_call" | custom-call | tf_op jit(solution)/shard_map/pallas_call | solution.py:400
  54.4 0.9 %shard_map.87 = (bf16[256,384]{1,0:T(8,128)(2,1)}, f32[384,384]{1,0:T(8,128)}) custom-call(bf16[256,384]{1,0:T(8,128)(2,1)S(1)} %get-tuple-element.6.upd_ref, f32[384,384]{1,0:T(8,128)S(1)} %get-tuple-element.7.grad_ref), custom_call_target="tpu_custom_call" | custom-call | tf_op jit(solution)/shard_map/pallas_call | solution.py:436

commit v5 on v4

--- a/solution.py
+++ b/solution.py
@@ -107,7 +107,7 @@
     tok_hbm, cot_hbm, qkv_hbm, out_w_hbm, cond_hbm, scale_hbm, step_ref,
     upd_ref, grad_ref,
     tok, cot, qkv, out_w, cond, scale_ref, packed, halo, q_s, k_s, v_s, acc, att, early,
-    own, cross, sent, part, z1, gath,
+    own, cross, sent, summed, part, z1, gath,
     in_sem, halo_s, halo_r, cross_s, cross_r, s1, r1, sz1, rz1, s3, r3, s4, r4,
 ):
     dp, tile = lax.axis_index("dp"), lax.axis_index("tile")
@@ -295,15 +295,21 @@
     first = jnp.concatenate([grads[0], grads[1][0:64]], axis=0)
     second = jnp.concatenate([grads[1][64:128], grads[2]], axis=0)
     sent[...] = jnp.where(core == 0, second, first).astype(BF16)
-    over = pltpu.make_async_remote_copy(
-        src_ref=sent, dst_ref=cross, send_sem=cross_s, recv_sem=cross_r, device_id=partner, device_id_type=MESH,
-    )
-    over.start()
+    over = []
+    for i in range(2):
+        piece = pl.ds(i * (HALF // 2), HALF // 2)
+        over.append(pltpu.make_async_remote_copy(
+            src_ref=sent.at[piece], dst_ref=cross.at[piece], send_sem=cross_s.at[i], recv_sem=cross_r.at[i],
+            device_id=partner, device_id_type=MESH,
+        ))
+        over[i].start()
     own[...] = jnp.where(core == 0, first, second)
     for p in range(3):
         att[p, far_queries] = pairs[p]
-    over.wait()
-    sent[...] = (own[...] + cross[...].astype(F32)).astype(BF16)
+    for i in range(2):
+        piece = slice(i * (HALF // 2), (i + 1) * (HALF // 2))
+        over[i].wait_recv()
+        summed[piece] = (own[piece] + cross[piece].astype(F32)).astype(BF16)
 
     for i, j in STEPS:
         ox, oy = lax.rem(x + i, 4), lax.rem(y + j, 4)
@@ -312,7 +318,7 @@
         @pl.when(k < OWNERS)
         def _():
             pltpu.make_async_remote_copy(
-                src_ref=sent.at[pl.ds(pl.multiple_of(k * ROWS, ROWS), ROWS)], dst_ref=part.at[chip],
+                src_ref=summed.at[pl.ds(pl.multiple_of(k * ROWS, ROWS), ROWS)], dst_ref=part.at[chip],
                 send_sem=s1, recv_sem=r1, device_id=device(ox, oy, core, z), device_id_type=MESH,
             ).start()
 
@@ -328,7 +334,7 @@
 
     @pl.when(owns)
     def _():
-        part[chip] = sent[pl.ds(pl.multiple_of(mine * ROWS, ROWS), ROWS)]
+        part[chip] = summed[pl.ds(pl.multiple_of(mine * ROWS, ROWS), ROWS)]
         pltpu.make_async_copy(part.at[pl.ds(0, 15)], part.at[pl.ds(0, 15)], r1).wait()
         z1[z] = total_of(part, 16)
         for i in ALONG:
@@ -365,6 +371,8 @@
     given = pl.ds(pl.multiple_of((1 - core) * HALF, ROWS), HALF)
     grad_ref[given] = gath[given].astype(F32)
 
+    over[0].wait_send()
+    over[1].wait_send()
     pltpu.make_async_copy(half, half, s4).wait()
     for i, (dr, dc, _, _, _) in enumerate(SENDS):
         @pl.when(there(dr, dc))
@@ -373,13 +381,13 @@
 
     @pl.when(owns)
     def _():
-        pltpu.make_async_copy(sent.at[pl.ds(0, HALF - ROWS)], sent.at[pl.ds(0, HALF - ROWS)], s1).wait()
+        pltpu.make_async_copy(summed.at[pl.ds(0, HALF - ROWS)], summed.at[pl.ds(0, HALF - ROWS)], s1).wait()
         pltpu.make_async_copy(z1.at[pl.ds(0, 15)], z1.at[pl.ds(0, 15)], sz1).wait()
         pltpu.make_async_copy(part.at[pl.ds(0, 15)], part.at[pl.ds(0, 15)], s3).wait()
 
     @pl.when(jnp.logical_not(owns))
     def _():
-        pltpu.make_async_copy(sent, sent, s1).wait()
+        pltpu.make_async_copy(summed, summed, s1).wait()
 
 
 def hand_over(upd_ref, grad_ref, upd_hbm, grad_hbm, sems):
@@ -420,11 +428,12 @@
             pltpu.VMEM((HALF, CH), F32),
             pltpu.VMEM((HALF, CH), BF16),
             pltpu.VMEM((HALF, CH), BF16),
+            pltpu.VMEM((HALF, CH), BF16),
             pltpu.VMEM((16, ROWS, CH), BF16),
             pltpu.VMEM((16, ROWS, CH), BF16),
             pltpu.VMEM((CH, CH), BF16),
-            dma((6,)), dma(()), dma((8,)),
-        ] + [dma(())] * 7 + [dma((OWNERS,)), dma(()), dma(())],
+            dma((6,)), dma(()), dma((8,)), dma((2,)), dma((2,)),
+        ] + [dma(())] * 5 + [dma((OWNERS,)), dma(()), dma(())],
         compiler_params=pltpu.CompilerParams(collective_id=0, has_side_effects=True, vmem_limit_bytes=40 * 2**20),
     )(*(
         pltpu.with_memory_space_constraint(array, pltpu.HBM)

time: 55.4 us -> 55.4 us (level)
  no operation moved by 1% of the time
where the time goes in v5:
time: 55.4 us; the launch traced here: 55.3 us
  Pallas kernels  54 us (97%)
  between operations  1.28 us (2%)
    pallas_call x1, Pallas kernels, body(): pl.pallas_call(kernel, out_shape=(pltpu.VMEM((TOKENS, CH), BF16), pltpu.V...  53.1 us

profile of v5, /device:TPU:1, one launch (start us, length us, event | category | flops | bytes accessed | tf_op | source)
XLA Modules:
  0.0 55.3 jit_solution(5715654010787601949)
XLA Ops:
  1.3 53.1 %shard_map.86 = (bf16[256,384]{1,0:T(8,128)(2,1)S(1)}, f32[384,384]{1,0:T(8,128)S(1)}) custom-call(bf16[256,384]{1,0:T(8,128)(2,1)} %bitcast.3, bf16[256,384]{1,0:T(8,128)(2,1)} %bitcast.4, bf16[384,1152]{1,0:T(8,128)(2,1)} %qkv_hbm.1, bf16[384,384]{1,0:T(8,128)(2,1)} %out_w_hbm.1, bf16[256,384]{1,0:T(8,128)(2,1)} %cond_hbm.1, f32[6]{0:T(128)} %scale_hbm.1, ...), custom_call_target="tpu_custom_call" | custom-call | tf_op jit(solution)/shard_map/pallas_call | solution.py:408
  54.4 0.9 %shard_map.87 = (bf16[256,384]{1,0:T(8,128)(2,1)}, f32[384,384]{1,0:T(8,128)}) custom-call(bf16[256,384]{1,0:T(8,128)(2,1)S(1)} %get-tuple-element.6.upd_ref, f32[384,384]{1,0:T(8,128)S(1)} %get-tuple-element.7.grad_ref), custom_call_target="tpu_custom_call" | custom-call | tf_op jit(solution)/shard_map/pallas_call | solution.py:445
